TPU v7x, 32 devices: a whole 2x2x4 slice. The times are simulated.
32 devices in a mesh: groups: 2 (over x), hours: 8 (over z, y), units: 2 (over core).
Axes of the slice: x: 2, y: 2, z: 4, core: 2. Of those that a mesh axis runs over, the one named last changes fastest.
Arguments:
- unit_zone: int32 [1024], P('units'), may hold values from 0 to 63
- up_window: int32 [1024], P('units'), may hold values from 1 to 24
- down_window: int32 [1024], P('units'), may hold values from 1 to 24
- switchable: int32 [1024], P('units'), may hold values 0 or 1
- capacity: float32 [1024], P('units'), may hold values from 0.5 to 2
- fixed_cost: float32 [1024], P('units'), may hold values from 0.1 to 1
- start_cost: float32 [1024], P('units'), may hold values from 0.5 to 8
- fuel_cost: float32 [2048, 1024], P(('groups', 'units'), 'hours'), parts along dimension 0, may hold values from 0.3 to 3
- demand: float32 [128, 1024], P('groups', 'hours'), parts along dimension 0, may hold values from 15 to 35
- commit: float32 [2048, 1024], P(('groups', 'units'), 'hours'), parts along dimension 0, may hold values from 0 to 1
- output: float32 [2048, 1024], P(('groups', 'units'), 'hours'), parts along dimension 0, may hold values from 0 to 1.5
- startup: float32 [2048, 1024], P(('groups', 'units'), 'hours'), parts along dimension 0, may hold values from 0 to 0.3
- price: float32 [128, 1024], P('groups', 'hours'), parts along dimension 0, may hold values from -6 to 6
- link_dual: float32 [2048, 1024], P(('groups', 'units'), 'hours'), parts along dimension 0, may hold values from 0 to 1
- up_dual: float32 [2048, 1024], P(('groups', 'units'), 'hours'), parts along dimension 0, may hold values from 0 to 1
- down_dual: float32 [2048, 1024], P(('groups', 'units'), 'hours'), parts along dimension 0, may hold values from 0 to 1
Outputs:
- commit_out: float32 [2048, 1024], P(('groups', 'units'), 'hours'), parts along dimension 0
- output_out: float32 [2048, 1024], P(('groups', 'units'), 'hours'), parts along dimension 0
- startup_out: float32 [2048, 1024], P(('groups', 'units'), 'hours'), parts along dimension 0
- price_out: float32 [128, 1024], P('groups', 'hours'), parts along dimension 0
- link_out: float32 [2048, 1024], P(('groups', 'units'), 'hours'), parts along dimension 0
- up_out: float32 [2048, 1024], P(('groups', 'units'), 'hours'), parts along dimension 0
- down_out: float32 [2048, 1024], P(('groups', 'units'), 'hours'), parts along dimension 0
There are 2 independent parts, one for each index of `groups`. A program takes and returns all parts, laid end to end along the dimension named above; an argument that names none is the same for every part. Nothing has to cross between parts.
All inputs are finite; a program needn't handle non-finite values. No bound on the sum of `switchable` on one device may be relied on, other than what follows from the above.
Results may differ from a plain program's by a relative error of at most 0.0003.
Values sent between devices are 32-bit elements; how exact they have to be, the bound alone decides.
A program may use at most 64 MiB of HBM per device.

v0:
```python
import jax
import jax.numpy as jnp
from jax import lax
from jax.sharding import PartitionSpec as P

WIN = 24


step_scale = 0.015
epsilon = 1e-06


def passed_along(block, axis, distance):
    devices = range(lax.axis_size(axis))
    route = [((i - distance) % len(devices), i) for i in devices]
    return lax.ppermute(block, axis, route)


def project_segment(point_x, point_g, start_x, start_g, end_x, end_g):
    delta_x = end_x - start_x
    delta_g = end_g - start_g
    length = delta_x * delta_x + delta_g * delta_g
    along = (point_x - start_x) * delta_x + (point_g - start_g) * delta_g
    ratio = jnp.where(length > 0, along / jnp.where(length > 0, length, 1.0), 0.0)
    ratio = jnp.clip(ratio, 0.0, 1.0)
    near_x = start_x + ratio * delta_x
    near_g = start_g + ratio * delta_g
    gap_x = point_x - near_x
    gap_g = point_g - near_g
    return (near_x, near_g, gap_x * gap_x + gap_g * gap_g)


def project_pair(point_x, point_g, floor_commit, limit):
    zero = jnp.zeros_like(limit)
    unity = jnp.ones_like(limit)
    corners = (
        (floor_commit, zero),
        (unity, zero),
        (unity, limit),
        (floor_commit, limit * floor_commit),
    )
    best_x, best_g, best_d = project_segment(
        point_x, point_g, corners[0][0], corners[0][1], corners[1][0], corners[1][1]
    )
    for side in range(1, 4):
        other = corners[(side + 1) % 4]
        nearer_x, nearer_g, distance = project_segment(
            point_x, point_g, corners[side][0], corners[side][1], other[0], other[1]
        )
        closer = distance < best_d
        best_x = jnp.where(closer, nearer_x, best_x)
        best_g = jnp.where(closer, nearer_g, best_g)
        best_d = jnp.where(closer, distance, best_d)
    inside = (
        (point_x >= floor_commit)
        & (point_x <= 1.0)
        & (point_g >= 0.0)
        & (point_g <= limit * point_x)
    )
    return (jnp.where(inside, point_x, best_x), jnp.where(inside, point_g, best_g))


def constraint_rows(commit, startup, up_window, down_window):
    hours = commit.shape[1]
    past = passed_along((commit[:, hours - WIN :], startup[:, hours - WIN :]), "hours", 1)
    commit_long = jnp.concatenate([past[0], commit], axis=1)
    startup_long = jnp.concatenate([past[1], startup], axis=1)
    up_sum = jnp.zeros_like(commit)
    down_sum = jnp.zeros_like(commit)
    lagged = jnp.zeros_like(commit)
    for offset in range(WIN):
        moved = startup_long[:, WIN - offset : WIN - offset + hours]
        up_sum = up_sum + jnp.where(offset < up_window[:, None], moved, 0.0)
        down_sum = down_sum + jnp.where(offset < down_window[:, None], moved, 0.0)
        lagged = lagged + jnp.where(
            down_window[:, None] == offset + 1,
            commit_long[:, WIN - offset - 1 : WIN - offset - 1 + hours],
            0.0,
        )
    link = commit - commit_long[:, WIN - 1 : WIN - 1 + hours] - startup
    upper = up_sum - commit
    lower = down_sum + lagged - 1.0
    return (link, upper, lower)


def adjoint_terms(link_long, up_long, down_long, up_window, down_window, span):
    grad_commit = link_long[:, :span] - link_long[:, 1 : span + 1] - up_long[:, :span]
    grad_startup = -link_long[:, :span]
    for offset in range(WIN):
        grad_startup = grad_startup + jnp.where(
            offset < up_window[:, None], up_long[:, offset : offset + span], 0.0
        )
        grad_startup = grad_startup + jnp.where(
            offset < down_window[:, None], down_long[:, offset : offset + span], 0.0
        )
        grad_commit = grad_commit + jnp.where(
            down_window[:, None] == offset + 1, down_long[:, offset + 1 : offset + 1 + span], 0.0
        )
    return (grad_commit, grad_startup)


def adjoint_rims(link_dual, up_dual, down_dual, up_window, down_window):
    rims = passed_along((link_dual[:, :WIN], up_dual[:, :WIN], down_dual[:, :WIN]), "hours", -1)
    link_long = jnp.concatenate([link_dual, rims[0]], axis=1)
    up_long = jnp.concatenate([up_dual, rims[1]], axis=1)
    down_long = jnp.concatenate([down_dual, rims[2]], axis=1)
    return adjoint_terms(link_long, up_long, down_long, up_window, down_window, link_dual.shape[1])


def body(
    unit_zone,
    up_window,
    down_window,
    switchable,
    capacity,
    fixed_cost,
    start_cost,
    fuel_cost,
    demand,
    commit,
    output,
    startup,
    price,
    link_dual,
    up_dual,
    down_dual,
):
    zones = price.shape[0]
    onehot = (unit_zone[None, :] == jnp.arange(zones, dtype=jnp.int32)[:, None]).astype(jnp.float32)
    floor_commit = (1 - switchable).astype(jnp.float32)[:, None]
    limit = capacity[:, None]
    weight = jnp.ones((), jnp.float32)
    for sweep in range(2):
        primal_step = step_scale / weight
        dual_step = step_scale * weight
        grad_commit, grad_startup = adjoint_rims(
            link_dual, up_dual, down_dual, up_window, down_window
        )
        grad_output = jnp.dot(onehot.T, price, precision=lax.Precision.HIGHEST)
        new_commit, new_output = project_pair(
            commit - primal_step * (fixed_cost[:, None] + grad_commit),
            output - primal_step * (fuel_cost + grad_output),
            floor_commit,
            limit,
        )
        new_startup = jnp.clip(
            startup - primal_step * (start_cost[:, None] + grad_startup), 0.0, 1.0
        )
        reflect_commit = 2.0 * new_commit - commit
        reflect_output = 2.0 * new_output - output
        reflect_startup = 2.0 * new_startup - startup
        link, upper, lower = constraint_rows(
            reflect_commit, reflect_startup, up_window, down_window
        )
        partial_value = jnp.dot(onehot, reflect_output, precision=lax.Precision.HIGHEST)
        total = lax.psum(partial_value, "units")
        new_price = price + dual_step * (total - demand)
        price_change = jnp.sum(jnp.square(new_price - price)) / lax.axis_size("units")
        new_link = jnp.maximum(link_dual + dual_step * link, 0.0)
        new_up = jnp.maximum(up_dual + dual_step * upper, 0.0)
        new_down = jnp.maximum(down_dual + dual_step * lower, 0.0)
        if sweep == 0:
            primal_change = (
                jnp.sum(jnp.square(new_commit - commit))
                + jnp.sum(jnp.square(new_output - output))
                + jnp.sum(jnp.square(new_startup - startup))
            )
            dual_change = (
                price_change
                + jnp.sum(jnp.square(new_link - link_dual))
                + jnp.sum(jnp.square(new_up - up_dual))
                + jnp.sum(jnp.square(new_down - down_dual))
            )
            changes = lax.psum((primal_change, dual_change), ("hours", "units"))
            weight = jnp.sqrt(jnp.sqrt((changes[1] + epsilon) / (changes[0] + epsilon)))
        commit, output, startup = (new_commit, new_output, new_startup)
        price, link_dual, up_dual, down_dual = (new_price, new_link, new_up, new_down)
    return (commit, output, startup, price, link_dual, up_dual, down_dual)


def solution(mesh):
    return jax.shard_map(
        body,
        mesh=mesh,
        in_specs=(
            P("units"),
            P("units"),
            P("units"),
            P("units"),
            P("units"),
            P("units"),
            P("units"),
            P(("groups", "units"), "hours"),
            P("groups", "hours"),
            P(("groups", "units"), "hours"),
            P(("groups", "units"), "hours"),
            P(("groups", "units"), "hours"),
            P("groups", "hours"),
            P(("groups", "units"), "hours"),
            P(("groups", "units"), "hours"),
            P(("groups", "units"), "hours"),
        ),
        out_specs=(
            P(("groups", "units"), "hours"),
            P(("groups", "units"), "hours"),
            P(("groups", "units"), "hours"),
            P("groups", "hours"),
            P(("groups", "units"), "hours"),
            P(("groups", "units"), "hours"),
            P(("groups", "units"), "hours"),
        ),
        check_vma=False,
    )
```

profile of v0, /device:TPU:0, one launch (start us, length us, event | category | flops | bytes accessed | tf_op | source)
XLA Modules:
  0.0 114.4 jit_solution(10344904547106246424)
XLA Ops:
  0.6 1.1 copy.28
  1.8 6.1 %collective-permute-start.1 = (f32[512,24]{0,1:T(8,128)S(1)}, f32[512,24]{0,1:T(8,128)S(1)}, u32[]{:S(2)}, u32[]{:S(2)}) collective-permute-start(f32[512,24]{0,1:T(8,128)S(1)} %slice.849), channel_id=1, source_target_pairs={{2,0},{4,2},{6,4},{8,6},{10,8},{12,10},{14,12},{0,14},{3,1},{5,3},... | collective-permute-start | bytes 147464 | tf_op jit(solution)/shard_map/ppermute | solution.py:16
  8.8 1.5 %collective-permute-start.3 = (f32[512,24]{0,1:T(8,128)S(1)}, f32[512,24]{0,1:T(8,128)S(1)}, u32[]{:S(2)}, u32[]{:S(2)}) collective-permute-start(f32[512,24]{0,1:T(8,128)S(1)} %slice.899), channel_id=1, source_target_pairs={{2,0},{4,2},{6,4},{8,6},{10,8},{12,10},{14,12},{0,14},{3,1},{5,3},... | collective-permute-start | bytes 147464 | tf_op jit(solution)/shard_map/ppermute | solution.py:16
  14.5 0.8 copy-done.3
  15.5 0.8 copy-done.4
  16.4 0.8 copy-done.5
  18.1 3.9 %multiply_reduce_fusion = (f32[]{:T(128)}, f32[512,128]{0,1:T(8,128)S(1)}) fusion(f32[512,128]{0,1:T(8,128)S(1)} %copy.39, pred[512]{0:T(512)(128)(4,1)S(1)} %get-tuple-element.85, f32[512,24]{0,1:T(8,128)S(1)} %collective-permute-done.3, f32[512,128]{0,1:T(8,128)S(1)} %copy.26, pred[512]{0:T(512)(128)(4,1)} %get-tuple-element.119, ...), kind=kLoop, calls=%fused_computation.886 | loop fusion | flops 9830399 | bytes 1435652 | tf_op jit(solution)/shard_map/reduce_sum | solution.py:166
  22.1 0.8 collective-permute-start.4
  22.9 0.7 copy-done.7
  23.6 4.5 %multiply_reduce_fusion.1 = (f32[]{:T(128)}, f32[512,128]{0,1:T(8,128)S(1)}, f32[512,128]{0,1:T(8,128)S(1)}, f32[512,128]{0,1:T(8,128)S(1)}) fusion(f32[512,128]{0,1:T(8,128)S(1)} %copy.31, f32[512]{0:T(512)S(1)} %get-tuple-element.92, f32[512]{0:T(512)S(1)} %get-tuple-element.91, pred[512]{0:T(512)(128)(4,1)} %get-tuple-element.88, ...), kind=kOutput, calls=%fused_computation.887 | convolution fusion | flops 61046784 | bytes 2533380 | tf_op jit(solution)/shard_map/dot_general | solution.py:139
  28.1 2.0 %multiply_reduce_fusion.2 = (f32[]{:T(128)}, f32[512,128]{0,1:T(8,128)S(1)}) fusion(f32[512,128]{0,1:T(8,128)S(1)} %copy.29, f32[512,128]{0,1:T(8,128)S(1)} %get-tuple-element.26, f32[512,128]{0,1:T(8,128)S(1)} %get-tuple-element.121, f32[512]{0:T(512)S(1)} %get-tuple-element.92, f32[512]{0:T(512)S(1)} %get-tuple-element.91, ...), kind=kLoop, calls=%fused_computation.888 | loop fusion | flops 5373951 | bytes 1075204 | tf_op jit(solution)/shard_map/reduce_sum | solution.py:164
  30.5 3.4 %psum.28 = f32[64,128]{1,0:T(8,128)S(1)} all-reduce(f32[64,128]{1,0:T(8,128)S(1)} %fusion.493), channel_id=1, replica_groups=mesh['groups'=2,'hours'=8,'units'=2] {'units'}, use_global_device_ids=true, to_apply=%region_0.1 | all-reduce | flops 8192 | bytes 65536 | tf_op jit(solution)/shard_map/psum | solution.py:156
  34.6 2.1 %multiply_reduce_fusion.4 = (f32[]{:T(128)}, f32[512,128]{0,1:T(8,128)S(1)}, f32[512,128]{0,1:T(8,128)S(1)}) fusion(f32[512,128]{0,1:T(8,128)S(1)} %copy.26, f32[512,128]{0,1:T(8,128)S(1)} %multiply_subtract_fusion.2, f32[512,24]{0,1:T(8,128)S(1)} %collective-permute-done.4, pred[512]{0:T(512)(128)(4,1)} %get-tuple-element.119, ...), kind=kLoop, calls=%fused_computation.890 | loop fusion | flops 5177343 | bytes 1634308 | tf_op jit(solution)/shard_map/reduce_sum | solution.py:171
  36.8 2.3 %collective-permute-start.2 = (f32[512,24]{0,1:T(8,128)S(1)}, f32[512,24]{0,1:T(8,128)S(1)}, u32[]{:S(2)}, u32[]{:S(2)}) collective-permute-start(f32[512,24]{0,1:T(8,128)S(1)} %slice.896), channel_id=1, source_target_pairs={{14,0},{0,2},{2,4},{4,6},{6,8},{8,10},{10,12},{12,14},{15,1},{1,3}... | collective-permute-start | bytes 147464 | tf_op jit(solution)/shard_map/ppermute | solution.py:16
  42.5 2.5 %collective-permute-start.7 = (f32[512,24]{0,1:T(8,128)S(1)}, f32[512,24]{0,1:T(8,128)S(1)}, u32[]{:S(2)}, u32[]{:S(2)}) collective-permute-start(f32[512,24]{0,1:T(8,128)S(1)} %slice.1081), channel_id=1, source_target_pairs={{2,0},{4,2},{6,4},{8,6},{10,8},{12,10},{14,12},{0,14},{3,1},{5,3},... | collective-permute-start | bytes 147464 | tf_op jit(solution)/shard_map/ppermute | solution.py:16
  45.2 3.8 %multiply_reduce_fusion.3 = (f32[]{:T(128)}, f32[512,128]{0,1:T(8,128)S(1)}) fusion(f32[512,128]{0,1:T(8,128)S(1)} %copy.28, f32[512,128]{0,1:T(8,128)S(1)} %get-tuple-element.33, f32[512,24]{0,1:T(8,128)S(1)} %collective-permute-done.2, pred[512]{0:T(512)(128)(4,1)} %get-tuple-element.62, pred[512]{0:T(512)(128)(4,1)} %get-tuple-element.63, ...), kind=kLoop, calls=%fused_computation.889 | loop fusion | flops 9764863 | bytes 1171460 | tf_op jit(solution)/shard_map/reduce_sum | solution.py:172
  49.0 1.3 %collective-permute-start.6 = (f32[512,24]{0,1:T(8,128)S(1)}, f32[512,24]{0,1:T(8,128)S(1)}, u32[]{:S(2)}, u32[]{:S(2)}) collective-permute-start(f32[512,24]{0,1:T(8,128)S(1)} %slice.1034), channel_id=1, source_target_pairs={{2,0},{4,2},{6,4},{8,6},{10,8},{12,10},{14,12},{0,14},{3,1},{5,3},... | collective-permute-start | bytes 147464 | tf_op jit(solution)/shard_map/ppermute | solution.py:16
  50.2 0.7 multiply_reduce_fusion.5
  52.8 30.0 %all-reduce = (f32[]{:T(128)}, f32[]{:T(128)}) all-reduce(f32[]{:T(128)S(6)} %add.1218, f32[]{:T(128)S(6)} %add.1221), channel_id=1, replica_groups=mesh['groups'=2,'hours'=8,'units'=2] {'hours','units'}, use_global_device_ids=true, to_apply=%region_5.6 | all-reduce | flops 2 | bytes 16 | tf_op jit(solution)/shard_map/psum | solution.py:174
  84.4 3.4 %multiply_subtract_fusion = (f32[512,128]{0,1:T(8,128)S(1)}, f32[512,128]{0,1:T(8,128)S(1)}) fusion(f32[512,128]{0,1:T(8,128)S(1)} %get-tuple-element.23, pred[512]{0:T(512)(128)(4,1)S(1)} %copy-done.79, f32[512,24]{0,1:T(8,128)S(1)} %collective-permute-done.7, f32[512,128]{0,1:T(8,128)S(1)} %get-tuple-element.32, pred[512]{0:T(512)(128)(4,1)} %get-tuple-element.119, ...), kind=kLoop, calls=%fused_computation.864 | loop fusion | flops 9764864 | bytes 1697796 | tf_op jit(solution)/shard_map/sub | solution.py:151
  87.9 2.3 %collective-permute-start.9 = (f32[512,24]{0,1:T(8,128)S(1)}, f32[512,24]{0,1:T(8,128)S(1)}, u32[]{:S(2)}, u32[]{:S(2)}) collective-permute-start(f32[512,24]{0,1:T(8,128)S(1)} %slice.1129), channel_id=1, source_target_pairs={{14,0},{0,2},{2,4},{4,6},{6,8},{8,10},{10,12},{12,14},{15,1},{1,3}... | collective-permute-start | bytes 147464 | tf_op jit(solution)/shard_map/ppermute | solution.py:16
  90.3 0.8 copy.53
  91.1 3.8 %collective-permute-done.9 = f32[512,24]{0,1:T(8,128)S(1)} collective-permute-done((f32[512,24]{0,1:T(8,128)S(1)}, f32[512,24]{0,1:T(8,128)S(1)}, u32[]{:S(2)}, u32[]{:S(2)}) %collective-permute-start.9) | collective-permute-done | bytes 49184 | tf_op jit(solution)/shard_map/ppermute | solution.py:16
  95.1 5.6 %add_maximum_fusion = (f32[512,128]{0,1:T(8,128)S(1)}, f32[512,128]{0,1:T(8,128)S(1)}, f32[512,128]{0,1:T(8,128)}, f32[512,128]{0,1:T(8,128)S(1)}, f32[512,128]{0,1:T(8,128)S(1)}) fusion(f32[512,128]{0,1:T(8,128)S(1)} %get-tuple-element.32, f32[512,128]{0,1:T(8,128)S(1)} %get-tuple-element.20, f32[512,24]{0,1:T(8,128)S(1)} %collective-permute-done.9, ...), kind=kOutput, calls=%fused_computation.862 | convolution fusion | flops 65855488 | bytes 3446792 | tf_op jit(solution)/shard_map/dot_general | solution.py:139
  100.8 1.4 %select_select_fusion = f32[512,128]{0,1:T(8,128)S(1)} fusion(f32[512,128]{0,1:T(8,128)S(1)} %get-tuple-element.122, f32[512]{0:T(512)S(1)} %get-tuple-element.37, f32[512]{0:T(512)S(1)} %get-tuple-element.95, f32[512]{0:T(512)S(1)} %get-tuple-element.38, f32[512]{0:T(512)S(1)} %copy-done.13, f32[512,128]{0,1:T(8,128)S(1)} %get-tuple-element.19, ...), kind=kLoop, calls=%fused_computation.869 | loop fusion | flops 5177344 | bytes 813056 | tf_op jit(solution)/shard_map/jit(_where)/select_n | solution.py:60
  102.4 3.4 %psum.31 = f32[64,128]{1,0:T(8,128)S(1)} all-reduce(f32[64,128]{1,0:T(8,128)S(1)} %fusion.490), channel_id=1, replica_groups=mesh['groups'=2,'hours'=8,'units'=2] {'units'}, use_global_device_ids=true, to_apply=%region_10.11 | all-reduce | flops 8192 | bytes 65536 | tf_op jit(solution)/shard_map/psum | solution.py:156
  106.5 0.8 copy.52
  107.4 0.8 copy.51
  108.5 0.8 copy.55
  109.5 3.1 %fusion.244 = f32[512,128]{0,1:T(8,128)S(1)} fusion(f32[512,128]{0,1:T(8,128)S(1)} %get-tuple-element.30, f32[512,128]{0,1:T(8,128)S(1)} %get-tuple-element.17, f32[512,24]{0,1:T(8,128)S(1)} %collective-permute-done.8, f32[512,128]{0,1:T(8,128)S(1)} %get-tuple-element.20, f32[512,24]{0,1:T(8,128)S(1)} %copy-done.10, f32[]{:T(128)S(6)} %mul.432, ...), kind=kLoop, calls=%fused_computation.606 | loop fusion | flops 9568256 | bytes 1171460 | tf_op jit(solution)/shard_map/max | solution.py:161
  112.7 0.8 copy.56
  113.6 0.8 copy.54
  (309 shorter events, 8.8 us)
Async XLA Ops:
  0.6 7.2 %copy-start = (f32[512,128]{1,0:T(8,128)S(1)}, f32[512,128]{1,0:T(8,128)}, u32[]{:S(2)}) copy-start(f32[512,128]{1,0:T(8,128)} %param.29) | copy-start | bytes 786436
  1.8 6.8 %copy-start.1 = (f32[512,128]{1,0:T(8,128)S(1)}, f32[512,128]{1,0:T(8,128)}, u32[]{:S(2)}) copy-start(f32[512,128]{1,0:T(8,128)} %param.30) | copy-start | bytes 786436
  1.8 15.6 %collective-permute-start.1 = (f32[512,24]{0,1:T(8,128)S(1)}, f32[512,24]{0,1:T(8,128)S(1)}, u32[]{:S(2)}, u32[]{:S(2)}) collective-permute-start(f32[512,24]{0,1:T(8,128)S(1)} %slice.849), channel_id=1, source_target_pairs={{2,0},{4,2},{6,4},{8,6},{10,8},{12,10},{14,12},{0,14},{3,1},{5,3},... | collective-permute-start | bytes 147464 | tf_op jit(solution)/shard_map/ppermute | solution.py:16
  8.0 14.8 %collective-permute-start = (f32[512,24]{0,1:T(8,128)S(1)}, f32[512,24]{0,1:T(8,128)S(1)}, u32[]{:S(2)}, u32[]{:S(2)}) collective-permute-start(f32[512,24]{0,1:T(8,128)S(1)} %slice.848), channel_id=1, source_target_pairs={{2,0},{4,2},{6,4},{8,6},{10,8},{12,10},{14,12},{0,14},{3,1},{5,3},... | collective-permute-start | bytes 147464 | tf_op jit(solution)/shard_map/ppermute | solution.py:16
  8.8 8.6 %collective-permute-start.3 = (f32[512,24]{0,1:T(8,128)S(1)}, f32[512,24]{0,1:T(8,128)S(1)}, u32[]{:S(2)}, u32[]{:S(2)}) collective-permute-start(f32[512,24]{0,1:T(8,128)S(1)} %slice.899), channel_id=1, source_target_pairs={{2,0},{4,2},{6,4},{8,6},{10,8},{12,10},{14,12},{0,14},{3,1},{5,3},... | collective-permute-start | bytes 147464 | tf_op jit(solution)/shard_map/ppermute | solution.py:16
  10.9 6.5 %copy-start.21 = (pred[512]{0:T(512)(128)(4,1)}, pred[512]{0:T(512)(128)(4,1)S(1)}, u32[]{:S(2)}) copy-start(pred[512]{0:T(512)(128)(4,1)S(1)} %get-tuple-element.43) | copy-start | bytes 1540
  10.9 6.5 %copy-start.24 = (pred[512]{0:T(512)(128)(4,1)}, pred[512]{0:T(512)(128)(4,1)S(1)}, u32[]{:S(2)}) copy-start(pred[512]{0:T(512)(128)(4,1)S(1)} %get-tuple-element.44) | copy-start | bytes 1540
  10.9 6.5 %copy-start.27 = (pred[512]{0:T(512)(128)(4,1)}, pred[512]{0:T(512)(128)(4,1)S(1)}, u32[]{:S(2)}) copy-start(pred[512]{0:T(512)(128)(4,1)S(1)} %get-tuple-element.45) | copy-start | bytes 1540
  10.9 6.5 %copy-start.30 = (pred[512]{0:T(512)(128)(4,1)}, pred[512]{0:T(512)(128)(4,1)S(1)}, u32[]{:S(2)}) copy-start(pred[512]{0:T(512)(128)(4,1)S(1)} %get-tuple-element.46) | copy-start | bytes 1540
  10.9 6.5 %copy-start.33 = (pred[512]{0:T(512)(128)(4,1)}, pred[512]{0:T(512)(128)(4,1)S(1)}, u32[]{:S(2)}) copy-start(pred[512]{0:T(512)(128)(4,1)S(1)} %get-tuple-element.47) | copy-start | bytes 1540
  10.9 6.5 %copy-start.36 = (pred[512]{0:T(512)(128)(4,1)}, pred[512]{0:T(512)(128)(4,1)S(1)}, u32[]{:S(2)}) copy-start(pred[512]{0:T(512)(128)(4,1)S(1)} %get-tuple-element.48) | copy-start | bytes 1540
  11.0 6.5 %copy-start.39 = (pred[512]{0:T(512)(128)(4,1)}, pred[512]{0:T(512)(128)(4,1)S(1)}, u32[]{:S(2)}) copy-start(pred[512]{0:T(512)(128)(4,1)S(1)} %get-tuple-element.49) | copy-start | bytes 1540
  11.0 6.5 %copy-start.42 = (pred[512]{0:T(512)(128)(4,1)}, pred[512]{0:T(512)(128)(4,1)S(1)}, u32[]{:S(2)}) copy-start(pred[512]{0:T(512)(128)(4,1)S(1)} %get-tuple-element.50) | copy-start | bytes 1540
  11.0 6.5 %copy-start.45 = (pred[512]{0:T(512)(128)(4,1)}, pred[512]{0:T(512)(128)(4,1)S(1)}, u32[]{:S(2)}) copy-start(pred[512]{0:T(512)(128)(4,1)S(1)} %get-tuple-element.51) | copy-start | bytes 1540
  11.0 6.5 %copy-start.48 = (pred[512]{0:T(512)(128)(4,1)}, pred[512]{0:T(512)(128)(4,1)S(1)}, u32[]{:S(2)}) copy-start(pred[512]{0:T(512)(128)(4,1)S(1)} %get-tuple-element.52) | copy-start | bytes 1540
  11.0 6.5 %copy-start.51 = (pred[512]{0:T(512)(128)(4,1)}, pred[512]{0:T(512)(128)(4,1)S(1)}, u32[]{:S(2)}) copy-start(pred[512]{0:T(512)(128)(4,1)S(1)} %get-tuple-element.53) | copy-start | bytes 1540
  11.0 6.5 %copy-start.54 = (pred[512]{0:T(512)(128)(4,1)}, pred[512]{0:T(512)(128)(4,1)S(1)}, u32[]{:S(2)}) copy-start(pred[512]{0:T(512)(128)(4,1)S(1)} %get-tuple-element.54) | copy-start | bytes 1540
  11.0 6.5 %copy-start.57 = (pred[512]{0:T(512)(128)(4,1)}, pred[512]{0:T(512)(128)(4,1)S(1)}, u32[]{:S(2)}) copy-start(pred[512]{0:T(512)(128)(4,1)S(1)} %get-tuple-element.55) | copy-start | bytes 1540
  11.0 6.5 %copy-start.60 = (pred[512]{0:T(512)(128)(4,1)}, pred[512]{0:T(512)(128)(4,1)S(1)}, u32[]{:S(2)}) copy-start(pred[512]{0:T(512)(128)(4,1)S(1)} %get-tuple-element.56) | copy-start | bytes 1540
  11.0 6.5 %copy-start.63 = (pred[512]{0:T(512)(128)(4,1)}, pred[512]{0:T(512)(128)(4,1)S(1)}, u32[]{:S(2)}) copy-start(pred[512]{0:T(512)(128)(4,1)S(1)} %get-tuple-element.57) | copy-start | bytes 1540
  11.1 6.5 %copy-start.66 = (pred[512]{0:T(512)(128)(4,1)}, pred[512]{0:T(512)(128)(4,1)S(1)}, u32[]{:S(2)}) copy-start(pred[512]{0:T(512)(128)(4,1)S(1)} %get-tuple-element.58) | copy-start | bytes 1540
  11.1 6.5 %copy-start.69 = (pred[512]{0:T(512)(128)(4,1)}, pred[512]{0:T(512)(128)(4,1)S(1)}, u32[]{:S(2)}) copy-start(pred[512]{0:T(512)(128)(4,1)S(1)} %get-tuple-element.59) | copy-start | bytes 1540
  11.1 73.3 %copy-start.15 = (pred[512]{0:T(512)(128)(4,1)}, pred[512]{0:T(512)(128)(4,1)S(1)}, u32[]{:S(2)}) copy-start(pred[512]{0:T(512)(128)(4,1)S(1)} %get-tuple-element.40) | copy-start | bytes 1540
  11.1 73.3 %copy-start.17 = (pred[512]{0:T(512)(128)(4,1)}, pred[512]{0:T(512)(128)(4,1)S(1)}, u32[]{:S(2)}) copy-start(pred[512]{0:T(512)(128)(4,1)S(1)} %get-tuple-element.41) | copy-start | bytes 1540
  11.1 73.3 %copy-start.19 = (pred[512]{0:T(512)(128)(4,1)}, pred[512]{0:T(512)(128)(4,1)S(1)}, u32[]{:S(2)}) copy-start(pred[512]{0:T(512)(128)(4,1)S(1)} %get-tuple-element.42) | copy-start | bytes 1540
  22.1 11.9 %collective-permute-start.4 = (f32[512,24]{0,1:T(8,128)S(1)}, f32[512,24]{0,1:T(8,128)S(1)}, u32[]{:S(2)}, u32[]{:S(2)}) collective-permute-start(f32[512,24]{0,1:T(8,128)S(1)} %slice.944), channel_id=1, source_target_pairs={{14,0},{0,2},{2,4},{4,6},{6,8},{8,10},{10,12},{12,14},{15,1},{1,3}... | collective-permute-start | bytes 147464 | tf_op jit(solution)/shard_map/ppermute | solution.py:16
  36.8 8.2 %collective-permute-start.2 = (f32[512,24]{0,1:T(8,128)S(1)}, f32[512,24]{0,1:T(8,128)S(1)}, u32[]{:S(2)}, u32[]{:S(2)}) collective-permute-start(f32[512,24]{0,1:T(8,128)S(1)} %slice.896), channel_id=1, source_target_pairs={{14,0},{0,2},{2,4},{4,6},{6,8},{8,10},{10,12},{12,14},{15,1},{1,3}... | collective-permute-start | bytes 147464 | tf_op jit(solution)/shard_map/ppermute | solution.py:16
  42.5 41.9 %collective-permute-start.7 = (f32[512,24]{0,1:T(8,128)S(1)}, f32[512,24]{0,1:T(8,128)S(1)}, u32[]{:S(2)}, u32[]{:S(2)}) collective-permute-start(f32[512,24]{0,1:T(8,128)S(1)} %slice.1081), channel_id=1, source_target_pairs={{2,0},{4,2},{6,4},{8,6},{10,8},{12,10},{14,12},{0,14},{3,1},{5,3},... | collective-permute-start | bytes 147464 | tf_op jit(solution)/shard_map/ppermute | solution.py:16
  49.0 35.4 %collective-permute-start.6 = (f32[512,24]{0,1:T(8,128)S(1)}, f32[512,24]{0,1:T(8,128)S(1)}, u32[]{:S(2)}, u32[]{:S(2)}) collective-permute-start(f32[512,24]{0,1:T(8,128)S(1)} %slice.1034), channel_id=1, source_target_pairs={{2,0},{4,2},{6,4},{8,6},{10,8},{12,10},{14,12},{0,14},{3,1},{5,3},... | collective-permute-start | bytes 147464 | tf_op jit(solution)/shard_map/ppermute | solution.py:16
  84.2 6.9 %collective-permute-start.5 = (f32[512,24]{0,1:T(8,128)S(1)}, f32[512,24]{0,1:T(8,128)}, u32[]{:S(2)}, u32[]{:S(2)}) collective-permute-start(f32[512,24]{0,1:T(8,128)S(1)} %slice.1033), channel_id=1, source_target_pairs={{2,0},{4,2},{6,4},{8,6},{10,8},{12,10},{14,12},{0,14},{3,1},{5,3},... | collective-permute-start | bytes 147464 | tf_op jit(solution)/shard_map/ppermute | solution.py:16
  87.9 7.0 %collective-permute-start.9 = (f32[512,24]{0,1:T(8,128)S(1)}, f32[512,24]{0,1:T(8,128)S(1)}, u32[]{:S(2)}, u32[]{:S(2)}) collective-permute-start(f32[512,24]{0,1:T(8,128)S(1)} %slice.1129), channel_id=1, source_target_pairs={{14,0},{0,2},{2,4},{4,6},{6,8},{8,10},{10,12},{12,14},{15,1},{1,3}... | collective-permute-start | bytes 147464 | tf_op jit(solution)/shard_map/ppermute | solution.py:16
  100.7 8.6 %collective-permute-start.8 = (f32[512,24]{0,1:T(8,128)S(1)}, f32[512,24]{0,1:T(8,128)S(1)}, u32[]{:S(2)}, u32[]{:S(2)}) collective-permute-start(f32[512,24]{0,1:T(8,128)S(1)} %slice.1126), channel_id=1, source_target_pairs={{14,0},{0,2},{2,4},{4,6},{6,8},{8,10},{10,12},{12,14},{15,1},{1,3}... | collective-permute-start | bytes 147464 | tf_op jit(solution)/shard_map/ppermute | solution.py:16
  (114 other events, 318.0 us)
where the time goes:
time: 115 us; the launch traced here: 114 us
  blocking collectives  36.8 us (32%)
  other arithmetic  24.3 us (21%)
  starting transfers between devices  17.3 us (15%)
  local copies, waits for them, and re-layouts  13 us (11%)
  matrix products  10.6 us (9%)
  between operations  8.6 us (7%)
  waiting for transfers between devices  3.81 us (3%)
    psum x1, blocking collectives, body(): changes = lax.psum((primal_change, dual_change), ('hours', 'units'))  30 us
    ppermute x10, starting transfers between devices, passed_along(): return lax.ppermute(block, axis, route)  17.3 us
    unnamed x285, local copies, waits for them, and re-layouts  12.9 us
    dot_general x2, matrix products, body(): grad_output = jnp.dot(onehot.T, price, precision=lax.Precision.HIGHEST)  10 us
    psum x2, blocking collectives, body(): total = lax.psum(partial_value, 'units')  6.81 us
    reduce_sum x1, other arithmetic, body(): jnp.sum(jnp.square(new_startup - startup))  3.94 us
    ppermute x10, waiting for transfers between devices, passed_along(): return lax.ppermute(block, axis, route)  3.81 us
    reduce_sum x1, other arithmetic, body(): jnp.sum(jnp.square(new_down - down_dual))  3.79 us
  transfers between devices with their start and end apart: 10, of which 1 were waited for; matrix products, arithmetic and copies ran while one was open for 25% of the time, Pallas kernels for 0%

commit v1 on v0

v1 whole, which is shorter than its diff:
```python
import functools

import jax
import jax.numpy as jnp
from jax import lax
from jax.experimental import pallas as pl
from jax.experimental.pallas import tpu as pltpu
from jax.sharding import PartitionSpec as P

WIN = 24
BITS = 5
LANES = 128
ROW = 8
FIRST = ROW + 2 * WIN

step_scale = 0.015
epsilon = 1e-06

MESH = pl.DeviceIdType.MESH


def later(x, k):
    return pltpu.roll(x, k, 0)


def sooner(x, k):
    return pltpu.roll(x, x.shape[0] - k, 0)


def bits_of(window, shape):
    wide = jnp.broadcast_to(window, shape)
    return [(wide & (1 << b)) != 0 for b in range(BITS)]


def doubled(x, move):
    sums = [x]
    for b in range(BITS - 1):
        sums.append(sums[-1] + move(sums[-1], 1 << b))
    return sums


def windowed(sums, bits, move, beyond=None):
    if beyond is None:
        total = jnp.where(bits[0], sums[0], 0.0)
    else:
        total = jnp.where(bits[0], sums[0] + move(beyond, 1), beyond)
    for b in range(1, BITS):
        total = jnp.where(bits[b], sums[b] + move(total, 1 << b), total)
    return total


def tile_sum(x):
    return jnp.sum(x.reshape(-1, ROW, x.shape[1]), axis=0)


def split_dot(a, b, dims, split_first):
    whole = a if split_first else b
    high = whole.astype(jnp.bfloat16)
    low = (whole - high.astype(jnp.float32)).astype(jnp.bfloat16)
    total = None
    for part in (high, low):
        pair = (part, b) if split_first else (a, part)
        term = lax.dot_general(*pair, (dims, ((), ())), preferred_element_type=jnp.float32)
        total = term if total is None else total + term
    return total


def kernel(
    n_hours,
    n_units,
    unit_zone,
    up_window,
    down_window,
    switchable,
    capacity,
    fixed_cost,
    start_cost,
    fuel_hbm,
    demand_hbm,
    commit_hbm,
    output_hbm,
    startup_hbm,
    price_hbm,
    link_hbm,
    up_hbm,
    down_hbm,
    commit_res,
    output_res,
    startup_res,
    price_res,
    link_res,
    up_res,
    down_res,
    inbuf,
    outbuf,
    price_v,
    demand_v,
    ipar,
    fpar,
    state,
    reflect,
    grads,
    send_first,
    halo_first,
    send_last,
    halo_last,
    partial,
    others,
    change,
    slots,
    in_sem,
    small_sem,
    out_sem,
    price_sem,
    sf_sem,
    rf_sem,
    sl_sem,
    rl_sem,
    sp_sem,
    rp_sem,
    sw_sem,
    rw_sem,
):
    hour = lax.axis_index("hours")
    unit = lax.axis_index("units")
    me = hour * n_units + unit
    n_all = n_hours * n_units
    following = lax.rem(hour + 1, n_hours)
    preceding = lax.rem(hour + n_hours - 1, n_hours)
    chunks = state.shape[1]
    span = state.shape[2]
    zones = price_v.shape[0]
    C, G, S, F, B, M, N = range(7)

    sources = (commit_hbm, output_hbm, startup_hbm, fuel_hbm, link_hbm, up_hbm, down_hbm)
    loads = [pltpu.make_async_copy(src, inbuf.at[i], in_sem.at[i]) for i, src in enumerate(sources)]
    price_load = pltpu.make_async_copy(price_hbm, price_v, small_sem.at[0])
    demand_load = pltpu.make_async_copy(demand_hbm, demand_v, small_sem.at[1])
    for i in (B, M, N, C, S, G, F):
        loads[i].start()
    price_load.start()
    demand_load.start()

    barrier = pltpu.get_barrier_semaphore()

    def greet(k, carry):
        peer = lax.rem(me + k, n_all)
        pl.semaphore_signal(
            barrier,
            inc=1,
            device_id={"hours": peer // n_units, "units": lax.rem(peer, n_units)},
            device_id_type=MESH,
        )
        return carry

    lax.fori_loop(1, n_all, greet, 0)

    for c in range(chunks):
        part = pl.ds(c * LANES, LANES)
        ipar[c, 0:1, :] = up_window[part].reshape(1, LANES)
        ipar[c, 1:2, :] = down_window[part].reshape(1, LANES)
        ipar[c, 2:3, :] = unit_zone[part].reshape(1, LANES)
        limit = capacity[part].reshape(1, LANES)
        fpar[c, 0:1, :] = limit
        fpar[c, 1:2, :] = 1.0 / (1.0 + limit * limit)
        fpar[c, 2:3, :] = jnp.where(switchable[part].reshape(1, LANES) == 0, 2.0, -3e38)
        fpar[c, 3:4, :] = fixed_cost[part].reshape(1, LANES)
        fpar[c, 4:5, :] = start_cost[part].reshape(1, LANES)

    def rows_of(c):
        return pl.ds(pl.multiple_of(c * LANES, LANES), LANES)

    def first_copy(sweep, c):
        return pltpu.make_async_remote_copy(
            src_ref=send_first.at[sweep, c],
            dst_ref=halo_first.at[sweep, c],
            send_sem=sf_sem.at[sweep, c],
            recv_sem=rf_sem.at[sweep, c],
            device_id={"hours": preceding},
            device_id_type=MESH,
        )

    def last_copy(sweep, c):
        return pltpu.make_async_remote_copy(
            src_ref=send_last.at[sweep, c],
            dst_ref=halo_last.at[sweep, c],
            send_sem=sl_sem.at[sweep, c],
            recv_sem=rl_sem.at[sweep, c],
            device_id={"hours": following},
            device_id_type=MESH,
        )

    def partial_copy(sweep, k):
        return pltpu.make_async_remote_copy(
            src_ref=partial.at[sweep],
            dst_ref=others.at[sweep, k - 1],
            send_sem=sp_sem.at[sweep, k - 1],
            recv_sem=rp_sem.at[sweep, k - 1],
            device_id={"units": lax.rem(unit + k, n_units)},
            device_id_type=MESH,
        )

    def put_first(sweep, c, link, up, down):
        send_first[sweep, c, 0:ROW, :] = link[0:ROW]
        send_first[sweep, c, ROW : ROW + WIN, :] = up[0:WIN]
        send_first[sweep, c, ROW + WIN : FIRST, :] = down[0:WIN]

    for i in (B, M, N):
        loads[i].wait()

    def turn_duals(c, carry):
        link, up, down = (inbuf[i, rows_of(c), :].T for i in (B, M, N))
        state[B, c] = link
        state[M, c] = up
        state[N, c] = down
        put_first(0, c, link, up, down)
        return carry

    lax.fori_loop(0, chunks, turn_duals, 0)
    pl.semaphore_wait(barrier, n_all - 1)

    def send_duals(c, carry):
        first_copy(0, c).start()
        return carry

    lax.fori_loop(0, chunks, send_duals, 0)
    for i in (C, S, G, F):
        loads[i].wait()

    def turn_rest(c, carry):
        for i in (C, G, S, F):
            state[i, c] = inbuf[i, rows_of(c), :].T
        return carry

    lax.fori_loop(0, chunks, turn_rest, 0)
    price_load.wait()
    demand_load.wait()
    change[...] = jnp.zeros_like(change)

    def onehot_of(c):
        rank = lax.broadcasted_iota(jnp.int32, (zones, LANES), 0)
        hit = rank == jnp.broadcast_to(ipar[c, 2:3, :], (zones, LANES))
        return jnp.where(hit, 1.0, 0.0).astype(jnp.bfloat16)

    def adjoint(sweep, c, carry):
        first_copy(sweep, c).wait_recv()
        link, up, down = (state[i, c] for i in (B, M, N))
        rim = halo_first.at[sweep, c]
        long = (span + WIN, LANES)
        up_bits = bits_of(ipar[c, 0:1, :], long)
        down_bits = bits_of(ipar[c, 1:2, :], long)
        up_long = jnp.concatenate([up, rim[ROW : ROW + WIN, :]], axis=0)
        total = windowed(doubled(up_long, sooner), up_bits, sooner)[:span] - link
        down_long = jnp.concatenate([down, rim[ROW + WIN : FIRST, :]], axis=0)
        total = total + windowed(doubled(down_long, sooner), down_bits, sooner)[:span]
        grads[1, c] = total
        lagged = down_long
        for b in range(BITS):
            lagged = jnp.where(down_bits[b], sooner(lagged, 1 << b), lagged)
        link_long = jnp.concatenate([link, rim[0:ROW, :]], axis=0)
        grads[0, c] = link - sooner(link_long, 1)[:span] - up + lagged[:span]
        return carry

    def primal(sweep, step, c, carry):
        limit = fpar[c, 0:1, :]
        onehot = onehot_of(c)
        commit, output, startup = (state[i, c] for i in (C, G, S))
        grad_output = split_dot(price_v[...], onehot, ((0,), (0,)), True)
        point_x = commit - step * (fpar[c, 3:4, :] + grads[0, c])
        point_g = output - step * (state[F, c] + grad_output)
        point_x = jnp.maximum(point_x, fpar[c, 2:3, :])
        above = point_g > limit * point_x
        ratio = jnp.clip((point_x + limit * point_g) * fpar[c, 1:2, :], 0.0, 1.0)
        new_commit = jnp.where(above, ratio, jnp.clip(point_x, 0.0, 1.0))
        new_output = jnp.where(above, limit * ratio, jnp.minimum(jnp.maximum(point_g, 0.0), limit))
        new_startup = jnp.clip(startup - step * (fpar[c, 4:5, :] + grads[1, c]), 0.0, 1.0)
        reflect_commit = 2.0 * new_commit - commit
        reflect_startup = 2.0 * new_startup - startup
        reflect[0, c] = reflect_commit
        reflect[1, c] = reflect_startup
        send_last[sweep, c, 0:WIN, :] = reflect_commit[span - WIN :]
        send_last[sweep, c, WIN:, :] = reflect_startup[span - WIN :]
        last_copy(sweep, c).start()
        reflect_output = 2.0 * new_output - output
        partial[sweep] += split_dot(onehot, reflect_output, ((1,), (1,)), False)
        if sweep == 0:
            change[0:ROW, :] += (
                tile_sum(jnp.square(new_commit - commit))
                + tile_sum(jnp.square(new_output - output))
                + tile_sum(jnp.square(new_startup - startup))
            )
            state[C, c] = new_commit
            state[G, c] = new_output
            state[S, c] = new_startup
        else:
            give(0, c, new_commit)
            give(1, c, new_output)
            give(2, c, new_startup)
        return carry

    results = (commit_res, output_res, startup_res, link_res, up_res, down_res)

    def store_of(i, c):
        return pltpu.make_async_copy(
            outbuf.at[i, rows_of(c), :], results[i].at[rows_of(c), :], out_sem.at[i, c]
        )

    def give(i, c, value):
        outbuf[i, rows_of(c), :] = value.T
        store_of(i, c).start()

    def rows(sweep, step, c, carry):
        last_copy(sweep, c).wait_recv()
        rim = halo_last.at[sweep, c]
        commit, startup = reflect[0, c], reflect[1, c]
        commit_long = jnp.concatenate([rim[0:WIN, :], commit], axis=0)
        startup_long = jnp.concatenate([rim[WIN:, :], startup], axis=0)
        long = (span + WIN, LANES)
        up_bits = bits_of(ipar[c, 0:1, :], long)
        down_bits = bits_of(ipar[c, 1:2, :], long)
        sums = doubled(startup_long, later)
        upper = windowed(sums, up_bits, later)[WIN:] - commit
        lower = windowed(sums, down_bits, later, commit_long)[WIN:] - 1.0
        link = commit - later(commit_long, 1)[WIN:] - startup
        olds = tuple(state[i, c] for i in (B, M, N))
        news = tuple(
            jnp.maximum(old + step * row, 0.0) for old, row in zip(olds, (link, upper, lower))
        )
        if sweep == 0:
            put_first(1, c, *news)
            first_copy(1, c).start()
            squares = [tile_sum(jnp.square(new - old)) for new, old in zip(news, olds)]
            change[ROW:, :] += squares[0] + squares[1] + squares[2]
            for i, new in zip((B, M, N), news):
                state[i, c] = new
        else:
            for i, new in enumerate(news):
                give(3 + i, c, new)
        return carry

    def totals(sweep):
        total = partial[sweep]
        for k in range(1, n_units):
            partial_copy(sweep, k).wait_recv()
            total = total + others[sweep, k - 1]
        return total

    def weight_copy(k):
        peer = lax.rem(me + k, n_all)
        return pltpu.make_async_remote_copy(
            src_ref=slots.at[me],
            dst_ref=slots.at[me],
            send_sem=sw_sem.at[k],
            recv_sem=rw_sem.at[me],
            device_id={"hours": peer // n_units, "units": lax.rem(peer, n_units)},
            device_id_type=MESH,
        )

    def weight_arrival(k):
        peer = lax.rem(me + k, n_all)
        return pltpu.make_async_remote_copy(
            src_ref=slots.at[peer],
            dst_ref=slots.at[peer],
            send_sem=sw_sem.at[k],
            recv_sem=rw_sem.at[peer],
            device_id={"hours": peer // n_units, "units": lax.rem(peer, n_units)},
            device_id_type=MESH,
        )

    primal_step = step_scale
    dual_step = step_scale
    for sweep in range(2):
        partial[sweep] = jnp.zeros((zones, span), jnp.float32)
        if sweep == 0:

            def both(c, carry):
                adjoint(0, c, 0)
                return primal(0, step_scale, c, carry)

            lax.fori_loop(0, chunks, both, 0)
        else:
            lax.fori_loop(0, chunks, functools.partial(adjoint, 1), 0)

            def send_done(k, carry):
                weight_arrival(k).wait_recv()
                return carry

            lax.fori_loop(1, n_all, send_done, 0)
            summed = jnp.sum(slots[...], axis=0)
            primal_change = jnp.sum(summed[:ROW], keepdims=True)
            dual_change = jnp.sum(summed[ROW:], keepdims=True)
            weight = jnp.sqrt(jnp.sqrt((dual_change + epsilon) / (primal_change + epsilon)))
            primal_step = jnp.broadcast_to(step_scale / weight, (1, LANES))
            dual_step = jnp.broadcast_to(step_scale * weight, (1, LANES))
            lax.fori_loop(0, chunks, functools.partial(primal, 1, primal_step), 0)
        for k in range(1, n_units):
            partial_copy(sweep, k).start()
        lax.fori_loop(0, chunks, functools.partial(rows, sweep, dual_step), 0)
        price = price_v[...]
        new_price = price + dual_step * (totals(sweep) - demand_v[...])
        price_v[...] = new_price
        if sweep == 0:
            change[ROW:, :] += tile_sum(jnp.square(new_price - price)) * (1.0 / n_units)
            slots[me] = change[...]

            def send_weight(k, carry):
                weight_copy(k).start()
                return carry

            lax.fori_loop(1, n_all, send_weight, 0)

    price_store = pltpu.make_async_copy(price_v, price_res, price_sem)
    price_store.start()

    def finish(c, carry):
        for sweep in range(2):
            first_copy(sweep, c).wait_send()
            last_copy(sweep, c).wait_send()
        for i in range(6):
            store_of(i, c).wait()
        return carry

    lax.fori_loop(0, chunks, finish, 0)
    for sweep in range(2):
        for k in range(1, n_units):
            partial_copy(sweep, k).wait_send()

    def finish_weight(k, carry):
        weight_copy(k).wait_send()
        return carry

    lax.fori_loop(1, n_all, finish_weight, 0)
    price_store.wait()


def body(*args):
    n_hours = lax.axis_size("hours")
    n_units = lax.axis_size("units")
    n_all = n_hours * n_units
    fuel_cost, demand = args[7], args[8]
    units, span = fuel_cost.shape
    zones = demand.shape[0]
    chunks = units // LANES
    f32 = jnp.float32
    wide = jax.ShapeDtypeStruct((units, span), f32)
    small = jax.ShapeDtypeStruct((zones, span), f32)
    vmem = pl.BlockSpec(memory_space=pltpu.VMEM)
    anywhere = pl.BlockSpec(memory_space=pl.ANY)
    dma = pltpu.SemaphoreType.DMA
    peers = max(n_units - 1, 1)
    return pl.pallas_call(
        functools.partial(kernel, n_hours, n_units),
        out_shape=(wide, wide, wide, small, wide, wide, wide),
        in_specs=[vmem] * 7 + [anywhere] * 9,
        out_specs=[anywhere] * 7,
        scratch_shapes=[
            pltpu.VMEM((7, units, span), f32),
            pltpu.VMEM((6, units, span), f32),
            pltpu.VMEM((zones, span), f32),
            pltpu.VMEM((zones, span), f32),
            pltpu.VMEM((chunks, ROW, LANES), jnp.int32),
            pltpu.VMEM((chunks, ROW, LANES), f32),
            pltpu.VMEM((7, chunks, span, LANES), f32),
            pltpu.VMEM((2, chunks, span, LANES), f32),
            pltpu.VMEM((2, chunks, span, LANES), f32),
            pltpu.VMEM((2, chunks, FIRST, LANES), f32),
            pltpu.VMEM((2, chunks, FIRST, LANES), f32),
            pltpu.VMEM((2, chunks, 2 * WIN, LANES), f32),
            pltpu.VMEM((2, chunks, 2 * WIN, LANES), f32),
            pltpu.VMEM((2, zones, span), f32),
            pltpu.VMEM((2, peers, zones, span), f32),
            pltpu.VMEM((2 * ROW, LANES), f32),
            pltpu.VMEM((n_all, 2 * ROW, LANES), f32),
            dma((7,)),
            dma((2,)),
            dma((6, chunks)),
            dma,
            dma((2, chunks)),
            dma((2, chunks)),
            dma((2, chunks)),
            dma((2, chunks)),
            dma((2, peers)),
            dma((2, peers)),
            dma((n_all,)),
            dma((n_all,)),
        ],
        compiler_params=pltpu.CompilerParams(
            collective_id=0, has_side_effects=True, vmem_limit_bytes=24 * 1024 * 1024
        ),
    )(*args)


def solution(mesh):
    unit = P("units")
    wide = P(("groups", "units"), "hours")
    zonal = P("groups", "hours")
    return jax.shard_map(
        body,
        mesh=mesh,
        in_specs=(unit,) * 7 + (wide, zonal, wide, wide, wide, zonal, wide, wide, wide),
        out_specs=(wide, wide, wide, zonal, wide, wide, wide),
        check_vma=False,
    )
```

time: 115 us -> 50.3 us (0.44)
  blocking collectives: 36.8 us -> 0 us
  Pallas kernels: 0 us -> 31.2 us
  other arithmetic: 24.3 us -> 0 us
  starting transfers between devices: 17.3 us -> 0 us
  matrix products: 10.6 us -> 0 us
  between operations: 8.6 us -> 0.67 us
  local copies, waits for them, and re-layouts: 13 us -> 17.8 us
  waiting for transfers between devices: 3.81 us -> 0 us
    psum x3 -> x0, blocking collectives: 36.8 us -> none  [the longest x1 30 us: body(): changes = lax.psum((primal_change, dual_change), ('hours', 'units'))]
    pallas_call x0 -> x1, Pallas kernels: none -> 31.2 us  [body(): pl.pallas_call(functools.partial(kernel, n_hours, n_units), out_shape=(wi...]
    ppermute x10 -> x0, starting transfers between devices: 17.3 us -> none  [passed_along(): return lax.ppermute(block, axis, route)]
    reduce_sum x6 -> x0, other arithmetic: 13.2 us -> none  [the longest x1 3.94 us: body(): jnp.sum(jnp.square(new_startup - startup))]
    dot_general x4 -> x0, matrix products: 10.6 us -> none  [the longest x2 10 us: body(): grad_output = jnp.dot(onehot.T, price, precision=lax.Precision.HIGHEST)]
    unnamed x285 -> x39, local copies, waits for them, and re-layouts: 12.9 us -> 17.8 us
    ppermute x10 -> x0, waiting for transfers between devices: 3.81 us -> none  [passed_along(): return lax.ppermute(block, axis, route)]
    sub x3 -> x0, other arithmetic: 3.49 us -> none  [the longest x2 3.49 us: body(): reflect_startup = 2.0 * new_startup - startup]
  transfers between devices with their start and end apart: 10 -> 0, of which waited for: 1 -> 0; matrix products, arithmetic and copies ran while one was open for 25% -> 0% of each run, Pallas kernels for 0% -> 0%
where the time goes in v1:
time: 50.3 us; the launch traced here: 49.7 us
  Pallas kernels  31.2 us (62%)
  local copies, waits for them, and re-layouts  17.8 us (35%)
  between operations  0.67 us (1%)
    pallas_call x1, Pallas kernels, body(): pl.pallas_call(functools.partial(kernel, n_hours, n_units), out_shape=(wi...  31.2 us
    unnamed x39, local copies, waits for them, and re-layouts  17.8 us

profile of v1, /device:TPU:0, one launch (start us, length us, event | category | flops | bytes accessed | tf_op | source)
XLA Modules:
  0.0 49.7 jit_solution(10362329556265702920)
XLA Ops:
  0.6 0.0 copy-start
  0.6 0.9 %copy-done = f32[512,128]{1,0:T(8,128)S(1)} copy-done((f32[512,128]{1,0:T(8,128)S(1)}, f32[512,128]{1,0:T(8,128)}, u32[]{:S(2)}) %copy-start) | copy-done | bytes 262168
  1.6 0.0 copy-start.1
  1.6 0.9 %copy-done.1 = f32[512,128]{1,0:T(8,128)S(1)} copy-done((f32[512,128]{1,0:T(8,128)S(1)}, f32[512,128]{1,0:T(8,128)}, u32[]{:S(2)}) %copy-start.1) | copy-done | bytes 262168
  2.5 0.0 copy-start.2
  2.5 0.9 %copy-done.2 = f32[512,128]{1,0:T(8,128)S(1)} copy-done((f32[512,128]{1,0:T(8,128)S(1)}, f32[512,128]{1,0:T(8,128)}, u32[]{:S(2)}) %copy-start.2) | copy-done | bytes 262168
  3.5 0.0 copy-start.3
  3.5 0.9 %copy-done.3 = f32[512,128]{1,0:T(8,128)S(1)} copy-done((f32[512,128]{1,0:T(8,128)S(1)}, f32[512,128]{1,0:T(8,128)}, u32[]{:S(2)}) %copy-start.3) | copy-done | bytes 262168
  4.4 0.0 copy-start.4
  4.4 0.9 %copy-done.4 = f32[512,128]{1,0:T(8,128)S(1)} copy-done((f32[512,128]{1,0:T(8,128)S(1)}, f32[512,128]{1,0:T(8,128)}, u32[]{:S(2)}) %copy-start.4) | copy-done | bytes 262168
  5.4 0.0 copy-start.5
  5.4 0.9 %copy-done.5 = f32[512,128]{1,0:T(8,128)S(1)} copy-done((f32[512,128]{1,0:T(8,128)S(1)}, f32[512,128]{1,0:T(8,128)}, u32[]{:S(2)}) %copy-start.5) | copy-done | bytes 262168
  6.3 0.0 copy-start.6
  6.3 0.9 %copy-done.6 = f32[512,128]{1,0:T(8,128)S(1)} copy-done((f32[512,128]{1,0:T(8,128)S(1)}, f32[512,128]{1,0:T(8,128)}, u32[]{:S(2)}) %copy-start.6) | copy-done | bytes 262168
  7.3 0.0 copy-start.7
  7.3 0.8 %copy-done.7 = f32[64,128]{1,0:T(8,128)S(1)} copy-done((f32[64,128]{1,0:T(8,128)S(1)}, f32[64,128]{1,0:T(8,128)}, u32[]{:S(2)}) %copy-start.7) | copy-done | bytes 32792
  8.1 0.8 %copy-done.8 = f32[64,128]{1,0:T(8,128)S(1)} copy-done((f32[64,128]{1,0:T(8,128)S(1)}, f32[64,128]{1,0:T(8,128)}, u32[]{:S(2)}) %copy-start.8) | copy-done | bytes 32792
  8.8 0.7 %copy-done.9 = s32[512]{0:T(512)S(1)} copy-done((s32[512]{0:T(512)S(1)}, s32[512]{0:T(512)}, u32[]{:S(2)}) %copy-start.9) | copy-done | bytes 2072
  9.5 0.7 %copy-done.10 = s32[512]{0:T(512)S(1)} copy-done((s32[512]{0:T(512)S(1)}, s32[512]{0:T(512)}, u32[]{:S(2)}) %copy-start.10) | copy-done | bytes 2072
  10.2 0.7 %copy-done.11 = s32[512]{0:T(512)S(1)} copy-done((s32[512]{0:T(512)S(1)}, s32[512]{0:T(512)}, u32[]{:S(2)}) %copy-start.11) | copy-done | bytes 2072
  10.9 0.7 %copy-done.12 = s32[512]{0:T(512)S(1)} copy-done((s32[512]{0:T(512)S(1)}, s32[512]{0:T(512)}, u32[]{:S(2)}) %copy-start.12) | copy-done | bytes 2072
  11.5 0.7 %copy-done.13 = f32[512]{0:T(512)S(1)} copy-done((f32[512]{0:T(512)S(1)}, f32[512]{0:T(512)}, u32[]{:S(2)}) %copy-start.13) | copy-done | bytes 2072
  12.2 0.7 %copy-done.14 = f32[512]{0:T(512)S(1)} copy-done((f32[512]{0:T(512)S(1)}, f32[512]{0:T(512)}, u32[]{:S(2)}) %copy-start.14) | copy-done | bytes 2072
  12.9 0.7 %copy-done.15 = f32[512]{0:T(512)S(1)} copy-done((f32[512]{0:T(512)S(1)}, f32[512]{0:T(512)}, u32[]{:S(2)}) %copy-start.15) | copy-done | bytes 2072
  13.6 31.2 %shard_map.207 = (f32[512,128]{1,0:T(8,128)S(1)}, f32[512,128]{1,0:T(8,128)S(1)}, f32[512,128]{1,0:T(8,128)S(1)}, f32[64,128]{1,0:T(8,128)S(1)}, f32[512,128]{1,...) custom-call(s32[512]{0:T(512)S(1)} %copy-done.9, s32[512]{0:T(512)S(1)} %copy-done.10, s32[512]{0:T(512)S(1)} %copy-done.11, ...), custom_call_target="tpu_custom_call" | custom-call | tf_op jit(solution)/shard_map/pallas_call | solution.py:451
  44.8 0.7 %copy.30 = f32[512,128]{1,0:T(8,128)} copy(f32[512,128]{1,0:T(8,128)S(1)} %get-tuple-element.14) | data formatting | bytes 524288
  45.5 0.7 %copy.31 = f32[512,128]{1,0:T(8,128)} copy(f32[512,128]{1,0:T(8,128)S(1)} %get-tuple-element.15) | data formatting | bytes 524288
  46.2 0.7 %copy.32 = f32[512,128]{1,0:T(8,128)} copy(f32[512,128]{1,0:T(8,128)S(1)} %get-tuple-element.16) | data formatting | bytes 524288
  47.0 0.6 %copy.33 = f32[64,128]{1,0:T(8,128)} copy(f32[64,128]{1,0:T(8,128)S(1)} %get-tuple-element.17) | data formatting | bytes 65536
  47.6 0.7 %copy.34 = f32[512,128]{1,0:T(8,128)} copy(f32[512,128]{1,0:T(8,128)S(1)} %get-tuple-element.18) | data formatting | bytes 524288
  48.3 0.7 %copy.35 = f32[512,128]{1,0:T(8,128)} copy(f32[512,128]{1,0:T(8,128)S(1)} %get-tuple-element.19) | data formatting | bytes 524288
  49.0 0.7 %copy.36 = f32[512,128]{1,0:T(8,128)} copy(f32[512,128]{1,0:T(8,128)S(1)} %get-tuple-element.20) | data formatting | bytes 524288
  (8 shorter events, 0.0 us)
Async XLA Ops:
  0.6 1.0 %copy-start = (f32[512,128]{1,0:T(8,128)S(1)}, f32[512,128]{1,0:T(8,128)}, u32[]{:S(2)}) copy-start(f32[512,128]{1,0:T(8,128)} %fuel_hbm.1) | copy-start | bytes 786436
  1.6 0.9 %copy-start.1 = (f32[512,128]{1,0:T(8,128)S(1)}, f32[512,128]{1,0:T(8,128)}, u32[]{:S(2)}) copy-start(f32[512,128]{1,0:T(8,128)} %commit_hbm.1) | copy-start | bytes 786436
  2.5 0.9 %copy-start.2 = (f32[512,128]{1,0:T(8,128)S(1)}, f32[512,128]{1,0:T(8,128)}, u32[]{:S(2)}) copy-start(f32[512,128]{1,0:T(8,128)} %output_hbm.1) | copy-start | bytes 786436
  3.5 0.9 %copy-start.3 = (f32[512,128]{1,0:T(8,128)S(1)}, f32[512,128]{1,0:T(8,128)}, u32[]{:S(2)}) copy-start(f32[512,128]{1,0:T(8,128)} %startup_hbm.1) | copy-start | bytes 786436
  4.4 0.9 %copy-start.4 = (f32[512,128]{1,0:T(8,128)S(1)}, f32[512,128]{1,0:T(8,128)}, u32[]{:S(2)}) copy-start(f32[512,128]{1,0:T(8,128)} %link_hbm.1) | copy-start | bytes 786436
  5.4 0.9 %copy-start.5 = (f32[512,128]{1,0:T(8,128)S(1)}, f32[512,128]{1,0:T(8,128)}, u32[]{:S(2)}) copy-start(f32[512,128]{1,0:T(8,128)} %up_hbm.1) | copy-start | bytes 786436
  6.3 0.9 %copy-start.6 = (f32[512,128]{1,0:T(8,128)S(1)}, f32[512,128]{1,0:T(8,128)}, u32[]{:S(2)}) copy-start(f32[512,128]{1,0:T(8,128)} %down_hbm.1) | copy-start | bytes 786436
  7.3 0.8 %copy-start.7 = (f32[64,128]{1,0:T(8,128)S(1)}, f32[64,128]{1,0:T(8,128)}, u32[]{:S(2)}) copy-start(f32[64,128]{1,0:T(8,128)} %demand_hbm.1) | copy-start | bytes 98308
  8.1 0.8 %copy-start.8 = (f32[64,128]{1,0:T(8,128)S(1)}, f32[64,128]{1,0:T(8,128)}, u32[]{:S(2)}) copy-start(f32[64,128]{1,0:T(8,128)} %price_hbm.1) | copy-start | bytes 98308
  8.8 0.7 %copy-start.9 = (s32[512]{0:T(512)S(1)}, s32[512]{0:T(512)}, u32[]{:S(2)}) copy-start(s32[512]{0:T(512)} %unit_zone.1) | copy-start | bytes 6148
  9.5 0.7 %copy-start.10 = (s32[512]{0:T(512)S(1)}, s32[512]{0:T(512)}, u32[]{:S(2)}) copy-start(s32[512]{0:T(512)} %up_window.1) | copy-start | bytes 6148
  10.2 0.7 %copy-start.11 = (s32[512]{0:T(512)S(1)}, s32[512]{0:T(512)}, u32[]{:S(2)}) copy-start(s32[512]{0:T(512)} %down_window.1) | copy-start | bytes 6148
  10.9 0.7 %copy-start.12 = (s32[512]{0:T(512)S(1)}, s32[512]{0:T(512)}, u32[]{:S(2)}) copy-start(s32[512]{0:T(512)} %switchable.1) | copy-start | bytes 6148
  11.5 0.7 %copy-start.13 = (f32[512]{0:T(512)S(1)}, f32[512]{0:T(512)}, u32[]{:S(2)}) copy-start(f32[512]{0:T(512)} %capacity.1) | copy-start | bytes 6148
  12.2 0.7 %copy-start.14 = (f32[512]{0:T(512)S(1)}, f32[512]{0:T(512)}, u32[]{:S(2)}) copy-start(f32[512]{0:T(512)} %fixed_cost.1) | copy-start | bytes 6148
  12.9 0.7 %copy-start.15 = (f32[512]{0:T(512)S(1)}, f32[512]{0:T(512)}, u32[]{:S(2)}) copy-start(f32[512]{0:T(512)} %start_cost.1) | copy-start | bytes 6148

commit v2 on v1

--- a/solution.py
+++ b/solution.py
@@ -53,28 +53,27 @@
     return jnp.sum(x.reshape(-1, ROW, x.shape[1]), axis=0)
 
 
-def split_dot(a, b, dims, split_first):
-    whole = a if split_first else b
-    high = whole.astype(jnp.bfloat16)
-    low = (whole - high.astype(jnp.float32)).astype(jnp.bfloat16)
-    total = None
-    for part in (high, low):
-        pair = (part, b) if split_first else (a, part)
-        term = lax.dot_general(*pair, (dims, ((), ())), preferred_element_type=jnp.float32)
-        total = term if total is None else total + term
-    return total
+def zone_sums(onehot, values):
+    high = values.astype(jnp.bfloat16)
+    low = (values - high.astype(jnp.float32)).astype(jnp.bfloat16)
+    return lax.dot_general(
+        jnp.concatenate([onehot, onehot], axis=1),
+        jnp.concatenate([high, low], axis=1),
+        (((1,), (1,)), ((), ())),
+        preferred_element_type=jnp.float32,
+    )
 
 
 def kernel(
     n_hours,
     n_units,
-    unit_zone,
-    up_window,
-    down_window,
-    switchable,
-    capacity,
-    fixed_cost,
-    start_cost,
+    unit_zone_hbm,
+    up_window_hbm,
+    down_window_hbm,
+    switchable_hbm,
+    capacity_hbm,
+    fixed_cost_hbm,
+    start_cost_hbm,
     fuel_hbm,
     demand_hbm,
     commit_hbm,
@@ -84,16 +83,20 @@
     link_hbm,
     up_hbm,
     down_hbm,
-    commit_res,
-    output_res,
-    startup_res,
+    turned_hbm,
     price_res,
-    link_res,
-    up_res,
-    down_res,
+    unit_zone,
+    up_window,
+    down_window,
+    switchable,
+    capacity,
+    fixed_cost,
+    start_cost,
     inbuf,
-    outbuf,
+    turned,
     price_v,
+    price_parts,
+    onehots,
     demand_v,
     ipar,
     fpar,
@@ -110,6 +113,7 @@
     slots,
     in_sem,
     small_sem,
+    unit_sem,
     out_sem,
     price_sem,
     sf_sem,
@@ -136,7 +140,23 @@
     loads = [pltpu.make_async_copy(src, inbuf.at[i], in_sem.at[i]) for i, src in enumerate(sources)]
     price_load = pltpu.make_async_copy(price_hbm, price_v, small_sem.at[0])
     demand_load = pltpu.make_async_copy(demand_hbm, demand_v, small_sem.at[1])
-    for i in (B, M, N, C, S, G, F):
+    unit_pairs = (
+        (unit_zone_hbm, unit_zone),
+        (up_window_hbm, up_window),
+        (down_window_hbm, down_window),
+        (switchable_hbm, switchable),
+        (capacity_hbm, capacity),
+        (fixed_cost_hbm, fixed_cost),
+        (start_cost_hbm, start_cost),
+    )
+    unit_loads = [
+        pltpu.make_async_copy(src, dst, unit_sem.at[i]) for i, (src, dst) in enumerate(unit_pairs)
+    ]
+    for i in (B, M, N):
+        loads[i].start()
+    for load in unit_loads:
+        load.start()
+    for i in (C, S, G, F):
         loads[i].start()
     price_load.start()
     demand_load.start()
@@ -155,6 +175,65 @@
 
     lax.fori_loop(1, n_all, greet, 0)
 
+    def rows_of(c):
+        return pl.ds(pl.multiple_of(c * LANES, LANES), LANES)
+
+    def first_copy(sweep, c):
+        return pltpu.make_async_remote_copy(
+            src_ref=send_first.at[sweep, c],
+            dst_ref=halo_first.at[sweep, c],
+            send_sem=sf_sem.at[sweep, c],
+            recv_sem=rf_sem.at[sweep, c],
+            device_id={"hours": preceding},
+            device_id_type=MESH,
+        )
+
+    def last_copy(sweep, c):
+        return pltpu.make_async_remote_copy(
+            src_ref=send_last.at[sweep, c],
+            dst_ref=halo_last.at[sweep, c],
+            send_sem=sl_sem.at[sweep, c],
+            recv_sem=rl_sem.at[sweep, c],
+            device_id={"hours": following},
+            device_id_type=MESH,
+        )
+
+    def partial_copy(sweep, k):
+        return pltpu.make_async_remote_copy(
+            src_ref=partial.at[sweep],
+            dst_ref=others.at[sweep, k - 1],
+            send_sem=sp_sem.at[sweep, k - 1],
+            recv_sem=rp_sem.at[sweep, k - 1],
+            device_id={"units": lax.rem(unit + k, n_units)},
+            device_id_type=MESH,
+        )
+
+    def put_first(sweep, c, link, up, down):
+        send_first[sweep, c, 0:ROW, :] = link[0:ROW]
+        send_first[sweep, c, ROW : ROW + WIN, :] = up[0:WIN]
+        send_first[sweep, c, ROW + WIN : FIRST, :] = down[0:WIN]
+
+    for i in (B, M, N):
+        loads[i].wait()
+
+    def turn_duals(c, carry):
+        link, up, down = (inbuf[i, rows_of(c), :].T for i in (B, M, N))
+        state[B, c] = link
+        state[M, c] = up
+        state[N, c] = down
+        put_first(0, c, link, up, down)
+        return carry
+
+    lax.fori_loop(0, chunks, turn_duals, 0)
+    pl.semaphore_wait(barrier, n_all - 1)
+
+    def send_duals(c, carry):
+        first_copy(0, c).start()
+        return carry
+
+    lax.fori_loop(0, chunks, send_duals, 0)
+    for load in unit_loads:
+        load.wait()
     for c in range(chunks):
         part = pl.ds(c * LANES, LANES)
         ipar[c, 0:1, :] = up_window[part].reshape(1, LANES)
@@ -166,64 +245,11 @@
         fpar[c, 2:3, :] = jnp.where(switchable[part].reshape(1, LANES) == 0, 2.0, -3e38)
         fpar[c, 3:4, :] = fixed_cost[part].reshape(1, LANES)
         fpar[c, 4:5, :] = start_cost[part].reshape(1, LANES)
-
-    def rows_of(c):
-        return pl.ds(pl.multiple_of(c * LANES, LANES), LANES)
-
-    def first_copy(sweep, c):
-        return pltpu.make_async_remote_copy(
-            src_ref=send_first.at[sweep, c],
-            dst_ref=halo_first.at[sweep, c],
-            send_sem=sf_sem.at[sweep, c],
-            recv_sem=rf_sem.at[sweep, c],
-            device_id={"hours": preceding},
-            device_id_type=MESH,
-        )
-
-    def last_copy(sweep, c):
-        return pltpu.make_async_remote_copy(
-            src_ref=send_last.at[sweep, c],
-            dst_ref=halo_last.at[sweep, c],
-            send_sem=sl_sem.at[sweep, c],
-            recv_sem=rl_sem.at[sweep, c],
-            device_id={"hours": following},
-            device_id_type=MESH,
-        )
-
-    def partial_copy(sweep, k):
-        return pltpu.make_async_remote_copy(
-            src_ref=partial.at[sweep],
-            dst_ref=others.at[sweep, k - 1],
-            send_sem=sp_sem.at[sweep, k - 1],
-            recv_sem=rp_sem.at[sweep, k - 1],
-            device_id={"units": lax.rem(unit + k, n_units)},
-            device_id_type=MESH,
-        )
-
-    def put_first(sweep, c, link, up, down):
-        send_first[sweep, c, 0:ROW, :] = link[0:ROW]
-        send_first[sweep, c, ROW : ROW + WIN, :] = up[0:WIN]
-        send_first[sweep, c, ROW + WIN : FIRST, :] = down[0:WIN]
-
-    for i in (B, M, N):
-        loads[i].wait()
-
-    def turn_duals(c, carry):
-        link, up, down = (inbuf[i, rows_of(c), :].T for i in (B, M, N))
-        state[B, c] = link
-        state[M, c] = up
-        state[N, c] = down
-        put_first(0, c, link, up, down)
-        return carry
-
-    lax.fori_loop(0, chunks, turn_duals, 0)
-    pl.semaphore_wait(barrier, n_all - 1)
-
-    def send_duals(c, carry):
-        first_copy(0, c).start()
-        return carry
-
-    lax.fori_loop(0, chunks, send_duals, 0)
+        rank = lax.broadcasted_iota(jnp.int32, (zones, LANES), 0)
+        hit = rank == jnp.broadcast_to(ipar[c, 2:3, :], (zones, LANES))
+        onehot = jnp.where(hit, 1.0, 0.0).astype(jnp.bfloat16)
+        onehots[c, 0:zones, :] = onehot
+        onehots[c, zones:, :] = onehot
     for i in (C, S, G, F):
         loads[i].wait()
 
@@ -237,10 +263,11 @@
     demand_load.wait()
     change[...] = jnp.zeros_like(change)
 
-    def onehot_of(c):
-        rank = lax.broadcasted_iota(jnp.int32, (zones, LANES), 0)
-        hit = rank == jnp.broadcast_to(ipar[c, 2:3, :], (zones, LANES))
-        return jnp.where(hit, 1.0, 0.0).astype(jnp.bfloat16)
+    def part_price():
+        turned_price = price_v[...].T
+        high = turned_price.astype(jnp.bfloat16)
+        low = (turned_price - high.astype(jnp.float32)).astype(jnp.bfloat16)
+        price_parts[...] = jnp.concatenate([high, low], axis=1)
 
     def adjoint(sweep, c, carry):
         first_copy(sweep, c).wait_recv()
@@ -263,9 +290,8 @@
 
     def primal(sweep, step, c, carry):
         limit = fpar[c, 0:1, :]
-        onehot = onehot_of(c)
         commit, output, startup = (state[i, c] for i in (C, G, S))
-        grad_output = split_dot(price_v[...], onehot, ((0,), (0,)), True)
+        grad_output = jnp.dot(price_parts[...], onehots[c], preferred_element_type=jnp.float32)
         point_x = commit - step * (fpar[c, 3:4, :] + grads[0, c])
         point_g = output - step * (state[F, c] + grad_output)
         point_x = jnp.maximum(point_x, fpar[c, 2:3, :])
@@ -282,7 +308,7 @@
         send_last[sweep, c, WIN:, :] = reflect_startup[span - WIN :]
         last_copy(sweep, c).start()
         reflect_output = 2.0 * new_output - output
-        partial[sweep] += split_dot(onehot, reflect_output, ((1,), (1,)), False)
+        partial[sweep] += zone_sums(onehots[c, 0:zones, :], reflect_output)
         if sweep == 0:
             change[0:ROW, :] += (
                 tile_sum(jnp.square(new_commit - commit))
@@ -298,15 +324,11 @@
             give(2, c, new_startup)
         return carry
 
-    results = (commit_res, output_res, startup_res, link_res, up_res, down_res)
-
     def store_of(i, c):
-        return pltpu.make_async_copy(
-            outbuf.at[i, rows_of(c), :], results[i].at[rows_of(c), :], out_sem.at[i, c]
-        )
+        return pltpu.make_async_copy(turned.at[i, c], turned_hbm.at[i, c], out_sem.at[i, c])
 
     def give(i, c, value):
-        outbuf[i, rows_of(c), :] = value.T
+        turned[i, c] = value
         store_of(i, c).start()
 
     def rows(sweep, step, c, carry):
@@ -371,6 +393,7 @@
     dual_step = step_scale
     for sweep in range(2):
         partial[sweep] = jnp.zeros((zones, span), jnp.float32)
+        part_price()
         if sweep == 0:
 
             def both(c, carry):
@@ -409,6 +432,7 @@
 
             lax.fori_loop(1, n_all, send_weight, 0)
 
+
     price_store = pltpu.make_async_copy(price_v, price_res, price_sem)
     price_store.start()
 
@@ -430,6 +454,25 @@
         return carry
 
     lax.fori_loop(1, n_all, finish_weight, 0)
+    price_store.wait()
+
+
+def place(turned, price, *rest):
+    results, price_res, held, outbuf, load_sem, sem, price_sem = rest[:6], *rest[6:]
+    chunks = turned.shape[1]
+    loads = [pltpu.make_async_copy(turned.at[i], held.at[i], load_sem.at[i]) for i in range(6)]
+    stores = [pltpu.make_async_copy(outbuf.at[i], results[i], sem.at[i]) for i in range(6)]
+    for load in loads:
+        load.start()
+    price_store = pltpu.make_async_copy(price, price_res, price_sem)
+    price_store.start()
+    for i in range(6):
+        loads[i].wait()
+        for c in range(chunks):
+            outbuf[i, c * LANES : (c + 1) * LANES, :] = held[i, c].T
+        stores[i].start()
+    for store in stores:
+        store.wait()
     price_store.wait()
 
 
@@ -444,19 +487,21 @@
     f32 = jnp.float32
     wide = jax.ShapeDtypeStruct((units, span), f32)
     small = jax.ShapeDtypeStruct((zones, span), f32)
-    vmem = pl.BlockSpec(memory_space=pltpu.VMEM)
-    anywhere = pl.BlockSpec(memory_space=pl.ANY)
+    hbm = pl.BlockSpec(memory_space=pltpu.HBM)
     dma = pltpu.SemaphoreType.DMA
     peers = max(n_units - 1, 1)
-    return pl.pallas_call(
+    turned, price = pl.pallas_call(
         functools.partial(kernel, n_hours, n_units),
-        out_shape=(wide, wide, wide, small, wide, wide, wide),
-        in_specs=[vmem] * 7 + [anywhere] * 9,
-        out_specs=[anywhere] * 7,
+        out_shape=(jax.ShapeDtypeStruct((6, chunks, span, LANES), f32), small),
+        in_specs=[hbm] * 16,
+        out_specs=[hbm] * 2,
         scratch_shapes=[
+            *[pltpu.VMEM((units,), arg.dtype) for arg in args[:7]],
             pltpu.VMEM((7, units, span), f32),
-            pltpu.VMEM((6, units, span), f32),
+            pltpu.VMEM((6, chunks, span, LANES), f32),
             pltpu.VMEM((zones, span), f32),
+            pltpu.VMEM((span, 2 * zones), jnp.bfloat16),
+            pltpu.VMEM((chunks, 2 * zones, LANES), jnp.bfloat16),
             pltpu.VMEM((zones, span), f32),
             pltpu.VMEM((chunks, ROW, LANES), jnp.int32),
             pltpu.VMEM((chunks, ROW, LANES), f32),
@@ -473,6 +518,7 @@
             pltpu.VMEM((n_all, 2 * ROW, LANES), f32),
             dma((7,)),
             dma((2,)),
+            dma((7,)),
             dma((6, chunks)),
             dma,
             dma((2, chunks)),
@@ -485,9 +531,24 @@
             dma((n_all,)),
         ],
         compiler_params=pltpu.CompilerParams(
-            collective_id=0, has_side_effects=True, vmem_limit_bytes=24 * 1024 * 1024
+            collective_id=0, has_side_effects=True, vmem_limit_bytes=56 * 1024 * 1024
         ),
     )(*args)
+    commit, output, startup, link, up, down, price = pl.pallas_call(
+        place,
+        out_shape=(wide,) * 6 + (small,),
+        in_specs=[hbm] * 2,
+        out_specs=[hbm] * 7,
+        scratch_shapes=[
+            pltpu.VMEM((6, chunks, span, LANES), f32),
+            pltpu.VMEM((6, units, span), f32),
+            dma((6,)),
+            dma((6,)),
+            dma,
+        ],
+        compiler_params=pltpu.CompilerParams(vmem_limit_bytes=56 * 1024 * 1024),
+    )(turned, price)
+    return (commit, output, startup, price, link, up, down)
 
 
 def solution(mesh):

time: 50.3 us -> 33.2 us (0.66)
  local copies, waits for them, and re-layouts: 17.8 us -> 0 us
  Pallas kernels: 31.2 us -> 32.4 us
    unnamed x39 -> x0, local copies, waits for them, and re-layouts: 17.8 us -> none
    pallas_call x1 -> x2, Pallas kernels: 31.2 us -> 32.4 us  [the longest x1 29.8 us: body(): pl.pallas_call(functools.partial(kernel, n_hours, n_units), out_shape=(ja...]
where the time goes in v2:
time: 33.2 us; the launch traced here: 33.1 us
  Pallas kernels  32.4 us (98%)
  between operations  0.65 us (2%)
    pallas_call x1, Pallas kernels, body(): pl.pallas_call(functools.partial(kernel, n_hours, n_units), out_shape=(ja...  29.8 us
    pallas_call x1, Pallas kernels, body(): pl.pallas_call(place, out_shape=(wide,) * 6 + (small,), in_specs=[hbm] *...  2.58 us

profile of v2, /device:TPU:0, one launch (start us, length us, event | category | flops | bytes accessed | tf_op | source)
XLA Modules:
  0.0 33.1 jit_solution(1286956808890279770)
XLA Ops:
  0.6 29.8 %shard_map.207 = (f32[6,4,128,128]{3,2,1,0:T(8,128)}, f32[64,128]{1,0:T(8,128)}) custom-call(s32[512]{0:T(512)} %unit_zone_hbm.1, s32[512]{0:T(512)} %up_window_hbm.1, s32[512]{0:T(512)} %down_window_hbm.1, s32[512]{0:T(512)} %switchable_hbm.1, f32[512]{0:T(512)} %capacity_hbm.1, f32[512]{0:T(512)} %fixed_cost_hbm.1, f32[512]{0:T(512)} %start_cost_hbm.1, ...), custom_call_target="tpu_custom_call" | custom-call | tf_op jit(solution)/shard_map/pallas_call | solution.py:493
  30.5 2.6 %shard_map.208 = (f32[512,128]{1,0:T(8,128)}, f32[512,128]{1,0:T(8,128)}, f32[512,128]{1,0:T(8,128)}, f32[512,128]{1,0:T(8,128)}, f32[512,128]{1,0:T(8,128)}, /*index=5*/f32[512,128]{1,0:T(8,128)}, f32[64,128]{1,0:T(8,128)}) custom-call(f32[6,4,128,128]{3,2,1,0:T(8,128)} %get-tuple-element.16.turned, f32[64,128]{1,0:T(8,128)} %get-tuple-element.17.price), custom_call_target="tpu_custom_call" | custom-call | tf_op jit(solution)/shard_map/pallas_call | solution.py:537

commit v3 on v2

--- a/solution.py
+++ b/solution.py
@@ -53,15 +53,10 @@
     return jnp.sum(x.reshape(-1, ROW, x.shape[1]), axis=0)
 
 
-def zone_sums(onehot, values):
+def two_parts(values):
     high = values.astype(jnp.bfloat16)
     low = (values - high.astype(jnp.float32)).astype(jnp.bfloat16)
-    return lax.dot_general(
-        jnp.concatenate([onehot, onehot], axis=1),
-        jnp.concatenate([high, low], axis=1),
-        (((1,), (1,)), ((), ())),
-        preferred_element_type=jnp.float32,
-    )
+    return jnp.concatenate([high, low], axis=1)
 
 
 def kernel(
@@ -97,6 +92,8 @@
     price_v,
     price_parts,
     onehots,
+    spread,
+    output_parts,
     demand_v,
     ipar,
     fpar,
@@ -176,7 +173,7 @@
     lax.fori_loop(1, n_all, greet, 0)
 
     def rows_of(c):
-        return pl.ds(pl.multiple_of(c * LANES, LANES), LANES)
+        return pl.ds(c * LANES, LANES)
 
     def first_copy(sweep, c):
         return pltpu.make_async_remote_copy(
@@ -224,14 +221,16 @@
         put_first(0, c, link, up, down)
         return carry
 
-    lax.fori_loop(0, chunks, turn_duals, 0)
+    for c in range(chunks):
+        turn_duals(c, 0)
     pl.semaphore_wait(barrier, n_all - 1)
 
     def send_duals(c, carry):
         first_copy(0, c).start()
         return carry
 
-    lax.fori_loop(0, chunks, send_duals, 0)
+    for c in range(chunks):
+        send_duals(c, 0)
     for load in unit_loads:
         load.wait()
     for c in range(chunks):
@@ -258,16 +257,29 @@
             state[i, c] = inbuf[i, rows_of(c), :].T
         return carry
 
-    lax.fori_loop(0, chunks, turn_rest, 0)
+    for c in range(chunks):
+        turn_rest(c, 0)
     price_load.wait()
     demand_load.wait()
     change[...] = jnp.zeros_like(change)
 
-    def part_price():
-        turned_price = price_v[...].T
-        high = turned_price.astype(jnp.bfloat16)
-        low = (turned_price - high.astype(jnp.float32)).astype(jnp.bfloat16)
-        price_parts[...] = jnp.concatenate([high, low], axis=1)
+    def spread_price():
+        price_parts[...] = two_parts(price_v[...].T)
+        for c in range(chunks):
+            spread[c] = jnp.dot(price_parts[...], onehots[c], preferred_element_type=jnp.float32)
+
+    def gather_output(sweep):
+        total = None
+        for c in range(chunks):
+            onehot = onehots[c, 0:zones, :]
+            term = lax.dot_general(
+                jnp.concatenate([onehot, onehot], axis=1),
+                output_parts[c],
+                (((1,), (1,)), ((), ())),
+                preferred_element_type=jnp.float32,
+            )
+            total = term if total is None else total + term
+        partial[sweep] = total
 
     def adjoint(sweep, c, carry):
         first_copy(sweep, c).wait_recv()
@@ -291,9 +303,8 @@
     def primal(sweep, step, c, carry):
         limit = fpar[c, 0:1, :]
         commit, output, startup = (state[i, c] for i in (C, G, S))
-        grad_output = jnp.dot(price_parts[...], onehots[c], preferred_element_type=jnp.float32)
         point_x = commit - step * (fpar[c, 3:4, :] + grads[0, c])
-        point_g = output - step * (state[F, c] + grad_output)
+        point_g = output - step * (state[F, c] + spread[c])
         point_x = jnp.maximum(point_x, fpar[c, 2:3, :])
         above = point_g > limit * point_x
         ratio = jnp.clip((point_x + limit * point_g) * fpar[c, 1:2, :], 0.0, 1.0)
@@ -302,13 +313,12 @@
         new_startup = jnp.clip(startup - step * (fpar[c, 4:5, :] + grads[1, c]), 0.0, 1.0)
         reflect_commit = 2.0 * new_commit - commit
         reflect_startup = 2.0 * new_startup - startup
+        output_parts[c] = two_parts(2.0 * new_output - output)
         reflect[0, c] = reflect_commit
         reflect[1, c] = reflect_startup
         send_last[sweep, c, 0:WIN, :] = reflect_commit[span - WIN :]
         send_last[sweep, c, WIN:, :] = reflect_startup[span - WIN :]
         last_copy(sweep, c).start()
-        reflect_output = 2.0 * new_output - output
-        partial[sweep] += zone_sums(onehots[c, 0:zones, :], reflect_output)
         if sweep == 0:
             change[0:ROW, :] += (
                 tile_sum(jnp.square(new_commit - commit))
@@ -392,8 +402,7 @@
     primal_step = step_scale
     dual_step = step_scale
     for sweep in range(2):
-        partial[sweep] = jnp.zeros((zones, span), jnp.float32)
-        part_price()
+        spread_price()
         if sweep == 0:
 
             def both(c, carry):
@@ -416,6 +425,7 @@
             primal_step = jnp.broadcast_to(step_scale / weight, (1, LANES))
             dual_step = jnp.broadcast_to(step_scale * weight, (1, LANES))
             lax.fori_loop(0, chunks, functools.partial(primal, 1, primal_step), 0)
+        gather_output(sweep)
         for k in range(1, n_units):
             partial_copy(sweep, k).start()
         lax.fori_loop(0, chunks, functools.partial(rows, sweep, dual_step), 0)
@@ -502,6 +512,8 @@
             pltpu.VMEM((zones, span), f32),
             pltpu.VMEM((span, 2 * zones), jnp.bfloat16),
             pltpu.VMEM((chunks, 2 * zones, LANES), jnp.bfloat16),
+            pltpu.VMEM((chunks, span, LANES), f32),
+            pltpu.VMEM((chunks, span, 2 * LANES), jnp.bfloat16),
             pltpu.VMEM((zones, span), f32),
             pltpu.VMEM((chunks, ROW, LANES), jnp.int32),
             pltpu.VMEM((chunks, ROW, LANES), f32),

time: 33.2 us -> 33 us (level)
  no operation moved by 1% of the time
where the time goes in v3:
time: 33 us; the launch traced here: 32.9 us
  Pallas kernels  32.2 us (98%)
  between operations  0.65 us (2%)
    pallas_call x1, Pallas kernels, body(): pl.pallas_call(functools.partial(kernel, n_hours, n_units), out_shape=(ja...  29.6 us
    pallas_call x1, Pallas kernels, body(): pl.pallas_call(place, out_shape=(wide,) * 6 + (small,), in_specs=[hbm] *...  2.58 us

profile of v3, /device:TPU:0, one launch (start us, length us, event | category | flops | bytes accessed | tf_op | source)
XLA Modules:
  0.0 32.9 jit_solution(12364220311927009851)
XLA Ops:
  0.6 29.6 %shard_map.207 = (f32[6,4,128,128]{3,2,1,0:T(8,128)}, f32[64,128]{1,0:T(8,128)}) custom-call(s32[512]{0:T(512)} %unit_zone_hbm.1, s32[512]{0:T(512)} %up_window_hbm.1, s32[512]{0:T(512)} %down_window_hbm.1, s32[512]{0:T(512)} %switchable_hbm.1, f32[512]{0:T(512)} %capacity_hbm.1, f32[512]{0:T(512)} %fixed_cost_hbm.1, f32[512]{0:T(512)} %start_cost_hbm.1, ...), custom_call_target="tpu_custom_call" | custom-call | tf_op jit(solution)/shard_map/pallas_call | solution.py:503
  30.3 2.6 %shard_map.208 = (f32[512,128]{1,0:T(8,128)}, f32[512,128]{1,0:T(8,128)}, f32[512,128]{1,0:T(8,128)}, f32[512,128]{1,0:T(8,128)}, f32[512,128]{1,0:T(8,128)}, /*index=5*/f32[512,128]{1,0:T(8,128)}, f32[64,128]{1,0:T(8,128)}) custom-call(f32[6,4,128,128]{3,2,1,0:T(8,128)} %get-tuple-element.16.turned, f32[64,128]{1,0:T(8,128)} %get-tuple-element.17.price), custom_call_target="tpu_custom_call" | custom-call | tf_op jit(solution)/shard_map/pallas_call | solution.py:549

commit v4 on v3

--- a/solution.py
+++ b/solution.py
@@ -419,8 +419,8 @@
 
             lax.fori_loop(1, n_all, send_done, 0)
             summed = jnp.sum(slots[...], axis=0)
-            primal_change = jnp.sum(summed[:ROW], keepdims=True)
-            dual_change = jnp.sum(summed[ROW:], keepdims=True)
+            primal_change = jnp.sum(summed[0:1], keepdims=True)
+            dual_change = jnp.sum(summed[1:2], keepdims=True)
             weight = jnp.sqrt(jnp.sqrt((dual_change + epsilon) / (primal_change + epsilon)))
             primal_step = jnp.broadcast_to(step_scale / weight, (1, LANES))
             dual_step = jnp.broadcast_to(step_scale * weight, (1, LANES))
@@ -434,7 +434,8 @@
         price_v[...] = new_price
         if sweep == 0:
             change[ROW:, :] += tile_sum(jnp.square(new_price - price)) * (1.0 / n_units)
-            slots[me] = change[...]
+            slots[me, 0:1, :] = jnp.sum(change[:ROW, :], axis=0, keepdims=True)
+            slots[me, 1:2, :] = jnp.sum(change[ROW:, :], axis=0, keepdims=True)
 
             def send_weight(k, carry):
                 weight_copy(k).start()
@@ -527,7 +528,7 @@
             pltpu.VMEM((2, zones, span), f32),
             pltpu.VMEM((2, peers, zones, span), f32),
             pltpu.VMEM((2 * ROW, LANES), f32),
-            pltpu.VMEM((n_all, 2 * ROW, LANES), f32),
+            pltpu.VMEM((n_all, 2, LANES), f32),
             dma((7,)),
             dma((2,)),
             dma((7,)),

time: 33 us -> 31.8 us (0.964)
  Pallas kernels: 32.2 us -> 31 us
    pallas_call x1, Pallas kernels: 29.6 us -> 28.4 us  [body(): pl.pallas_call(functools.partial(kernel, n_hours, n_units), out_shape=(ja...]
where the time goes in v4:
time: 31.8 us; the launch traced here: 31.7 us
  Pallas kernels  31 us (97%)
  between operations  0.65 us (2%)
    pallas_call x1, Pallas kernels, body(): pl.pallas_call(functools.partial(kernel, n_hours, n_units), out_shape=(ja...  28.4 us
    pallas_call x1, Pallas kernels, body(): pl.pallas_call(place, out_shape=(wide,) * 6 + (small,), in_specs=[hbm] *...  2.58 us

profile of v4, /device:TPU:0, one launch (start us, length us, event | category | flops | bytes accessed | tf_op | source)
XLA Modules:
  0.0 31.7 jit_solution(7613169041993695918)
XLA Ops:
  0.6 28.4 %shard_map.207 = (f32[6,4,128,128]{3,2,1,0:T(8,128)}, f32[64,128]{1,0:T(8,128)}) custom-call(s32[512]{0:T(512)} %unit_zone_hbm.1, s32[512]{0:T(512)} %up_window_hbm.1, s32[512]{0:T(512)} %down_window_hbm.1, s32[512]{0:T(512)} %switchable_hbm.1, f32[512]{0:T(512)} %capacity_hbm.1, f32[512]{0:T(512)} %fixed_cost_hbm.1, f32[512]{0:T(512)} %start_cost_hbm.1, ...), custom_call_target="tpu_custom_call" | custom-call | tf_op jit(solution)/shard_map/pallas_call | solution.py:504
  29.1 2.6 %shard_map.208 = (f32[512,128]{1,0:T(8,128)}, f32[512,128]{1,0:T(8,128)}, f32[512,128]{1,0:T(8,128)}, f32[512,128]{1,0:T(8,128)}, f32[512,128]{1,0:T(8,128)}, /*index=5*/f32[512,128]{1,0:T(8,128)}, f32[64,128]{1,0:T(8,128)}) custom-call(f32[6,4,128,128]{3,2,1,0:T(8,128)} %get-tuple-element.16.turned, f32[64,128]{1,0:T(8,128)} %get-tuple-element.17.price), custom_call_target="tpu_custom_call" | custom-call | tf_op jit(solution)/shard_map/pallas_call | solution.py:550
